TPU v7x, 32 devices: a whole 2x2x4 slice. The times are simulated.
32 devices in a mesh: feat: 4 (over x, core), rows: 8 (over z, y).
Axes of the slice: x: 2, y: 2, z: 4, core: 2. Of those that a mesh axis runs over, the one named last changes fastest.
Arguments:
- features: bfloat16 [16, 2, 1024, 100], P('rows', None, None, 'feat'), may hold values from -6 to 6
- feature_masks: int32 [16, 100], P(None, 'feat'), may hold values from 0 to 1, as said below
- table_map: int32 [16], P('rows'), may hold values from 0 to 15, each once
- owners: int32 [24], replicated, may hold values from 0 to 7, as said below
- out_grad: bfloat16 [16, 2, 1024, 512], P('rows', None, 'feat'), may hold values from -6 to 6
- weight_slots: float32 [32, 256, 512], P('rows')
- moment1_slots: float32 [32, 256, 512], P('rows')
- moment2_slots: float32 [32, 256, 512], P('rows')
- emb_weight: float32 [100, 512], P('feat'), may hold values from -0.625 to 0.625
- emb_moment1: float32 [100, 512], P('feat')
- emb_moment2: float32 [100, 512], P('feat')
- small_weight: float32 [10, 512], replicated
- small_moment1: float32 [10, 512], replicated
- small_moment2: float32 [10, 512], replicated
Outputs:
- layer_out: bfloat16 [16, 2, 1024, 512], P('rows', None, 'feat')
- grad_inputs: bfloat16 [16, 2, 1024, 100], P('rows', None, None, 'feat')
- grad_slots: float32 [32, 256, 512], P('rows')
- moment1_out: float32 [32, 256, 512], P('rows')
- moment2_out: float32 [32, 256, 512], P('rows')
- weight_out: float32 [32, 256, 512], P('rows')
- weight_copies: bfloat16 [32, 256, 512], P('rows')
- emb_grad: float32 [100, 512], P('feat')
- emb_moment1_out: float32 [100, 512], P('feat')
- emb_moment2_out: float32 [100, 512], P('feat')
- emb_weight_out: float32 [100, 512], P('feat')
- emb_copy: bfloat16 [100, 512], P('feat')
- small_grad: float32 [10, 512], replicated
- small_moment1_out: float32 [10, 512], replicated
- small_moment2_out: float32 [10, 512], replicated
- small_weight_out: float32 [10, 512], replicated
Inputs may be any that keep to these rules, and one draw needn't show every extreme that they name: `feature_masks`: each row is 1 on the first k features and 0 on the rest, k from 2 to 100; some table has all 100. `table_map`: A permutation of the table numbers. `owners`: no index owns more than 4 blocks, and some own exactly 4.
All inputs are finite; a program needn't handle non-finite values.
Results may differ from a plain program's by a relative error of at most 0.015.
Values may be sent and summed in bfloat16 or wider, within the bound.
A program may use at most 192 MiB of HBM per device.

v0:
```python
import functools
import math

import jax
import jax.numpy as jnp
from jax import lax
from jax.experimental import pallas as pl
from jax.experimental.pallas import tpu as pltpu
from jax.sharding import PartitionSpec as P

MESH = pl.DeviceIdType.MESH
bf16, f32 = jnp.bfloat16, jnp.float32
NN = (((1,), (0,)), ((), ()))
NT = (((1,), (1,)), ((), ()))
TN = (((0,), (0,)), ((), ()))
LOG2E = math.log2(math.e)
HEADS = 4
HEAD_DIM = 128
STEP = 10
LN_EPS = 1e-05
BETA_FIRST = 0.9
BETA_SECOND = 0.999
ADAM_EPS = 1e-08
DECAY = 0.01
RATE_MATRIX = 0.1
RATE_EMBED = 0.3
RATE_SMALL = 0.6
D = 512
HALF = 1024
QUART = 256
PADF = 32
VMEM_BYTES = 60 * 2**20


def dot(a, b, dims=NN):
    return lax.dot_general(a, b, dims, preferred_element_type=f32)


def vmem():
    return pl.BlockSpec(memory_space=pltpu.VMEM)


def anyspace():
    return pl.BlockSpec(memory_space=pl.ANY)


def smem():
    return pl.BlockSpec(memory_space=pltpu.SMEM)


def remote(src, dst, send, recv, dev):
    return pltpu.make_async_remote_copy(
        src_ref=src, dst_ref=dst, send_sem=send, recv_sem=recv, device_id=dev, device_id_type=MESH
    )


def greet(peers):
    bar = pltpu.get_barrier_semaphore()
    for d in peers:
        pl.semaphore_signal(bar, inc=1, device_id=d, device_id_type=MESH)
    return bar


def mask_column(masks, table):
    T, nf = masks.shape
    which = lax.broadcasted_iota(jnp.int32, (T, nf), 0) == table
    line = jnp.sum(jnp.where(which, masks[...], 0), axis=0, keepdims=True)
    eye = lax.broadcasted_iota(jnp.int32, (nf, nf), 0) == lax.broadcasted_iota(jnp.int32, (nf, nf), 1)
    return jnp.sum(jnp.where(eye, jnp.broadcast_to(line, (nf, nf)), 0), axis=1, keepdims=True).astype(f32)


GROUPS = (True, False)


def gather_kernel(
    R, slots_ref, feat_ref, mask_ref, tmap_ref, own_ref, emb_ref, small_ref,
    su_ref, kind_ref, XT_ref, h0_ref, a1s_ref, a1q_ref, n1s_ref, n1q_ref, rs_ref, rq_ref, linv,
    Wo, qo, kTo, vo, ET, OT, Oo,
    pos, G0, G1, own, XTo, XTa, tmpq, W, q_s, k_s, kT_s, v_s, vT_s, ET_s, OT_s, O_s,
    lsem, osem, esem, fs, fr, hs, hr, xs, xr, cs, cr, c2s, c2r,
):
    f = lax.axis_index("feat")
    r = lax.axis_index("rows")
    x = f // 2
    c = f % 2
    n = R.bit_length() - 1
    S, BR = slots_ref.shape[:2]
    U = own_ref.shape[0]
    BH = BR // 2
    Gs = (G0, G1)
    core_id = (f ^ 1, r)
    x_id = (f ^ 2, r)
    row_id = [(f, r ^ (1 << (n - 1 - j))) for j in range(n)]
    peers = [core_id, x_id] + row_id
    bar = greet(peers)
    for k in range(4):
        own[k // 2, k % 2] = slots_ref[:, :, k * 128:(k + 1) * 128].astype(bf16)
    pl.semaphore_wait(bar, len(peers))

    def keep_own(p):
        return pltpu.make_async_copy(own.at[p], Gs[p].at[:, 0], lsem.at[p])

    subs = [(j, g) for j in range(n) for g in range(-1, j)]
    index = {jg: i for i, jg in enumerate(subs)}
    rows_c = pl.ds(pl.multiple_of(c * BH, BH), BH)

    def part(p, s, half, start, size):
        if GROUPS[s]:
            return Gs[p].at[half, pl.ds(start, size), pl.ds(1, 3), rows_c]
        return Gs[p].at[:, pl.ds(start, size), 0, rows_c]

    def hyper(p, s, j, g):
        k = index[(j, g)]
        if g < 0:
            if GROUPS[s]:
                src, dst = own.at[p, x, pl.ds(1, 3), rows_c], Gs[p].at[x, 1 << j, pl.ds(1, 3), rows_c]
            else:
                src, dst = own.at[p, :, 0, rows_c], Gs[p].at[:, 1 << j, 0, rows_c]
        else:
            src, dst = part(p, s, x, 1 << g, 1 << g), part(p, s, x, (1 << j) + (1 << g), 1 << g)
        return remote(src, dst, hs.at[p, s, k], hr.at[p, s, k], row_id[j])

    def forward(p, s, j, g, half, sems, semr, dev):
        start, size = (0, 1) if g < 0 else (1 << g, 1 << g)
        k = index[(j, g)]
        ref = part(p, s, half, (1 << j) + start, size)
        return remote(ref, ref, sems.at[p, s, k], semr.at[p, s, k], dev)

    def to_x(p, s, j, g):
        return forward(p, s, j, g, x, xs, xr, x_id)

    def to_core(p, s, j, g):
        return forward(p, s, j, g, x, cs, cr, core_id)

    def to_core_x(p, s, j, g):
        return forward(p, s, j, g, 1 - x, c2s, c2r, core_id)

    order = range(len(GROUPS))

    def send_own(p):
        for s in order:
            for j in range(n):
                hyper(p, s, j, -1).start()
        keep_own(p).start()

    def x_arrive(p, j):
        for s in order:
            if GROUPS[s]:
                for g in range(-1, j):
                    to_x(p, s, j, g).wait_recv()
                    to_core_x(p, s, j, g).start()

    def hyper_arrive(p, j):
        for s in order:
            for g in range(-1, j):
                hyper(p, s, j, g).wait_recv()
                if GROUPS[s]:
                    to_x(p, s, j, g).start()
                to_core(p, s, j, g).start()
            for j2 in range(j + 1, n):
                hyper(p, s, j2, j).start()

    def all_here(p):
        keep_own(p).wait()
        for s in order:
            for j, g in subs:
                to_core(p, s, j, g).wait_recv()
                if GROUPS[s]:
                    to_core_x(p, s, j, g).wait_recv()

    def all_sent(p):
        for s in order:
            for j, g in subs:
                hyper(p, s, j, g).wait_send()
                to_core(p, s, j, g).wait_send()
                if GROUPS[s]:
                    to_x(p, s, j, g).wait_send()
                    to_core_x(p, s, j, g).wait_send()

    send_own(0)

    nf = feat_ref.shape[1]
    XTo[...] = jnp.zeros_like(XTo)
    for t in range(2):
        keep = mask_column(mask_ref, tmap_ref[t])
        XTo[pl.ds(0, nf), pl.ds(t * HALF, HALF)] = (feat_ref[t, :, 0, :].astype(f32) * keep).astype(bf16)
        query = (feat_ref[t, :, 1, :].astype(f32) * keep).astype(bf16)
        for k in range(4):
            XTo[pl.ds(0, nf), pl.ds(2 * HALF + D + k * 512 + t * QUART, QUART)] = query[:, k * QUART:(k + 1) * QUART]
    XTo[pl.ds(0, nf), pl.ds(2 * HALF, D)] = emb_ref[...].astype(bf16)
    wide = 2 * HALF + D
    shared = pl.ds(0, wide)
    tail = pl.ds(wide, 512)

    def rows_of(dev):
        return pl.ds(pl.multiple_of(dev * PADF, PADF), PADF)

    def chunk_of(dev):
        return pl.ds(pl.multiple_of(wide + dev * 512, 512), 512)

    feats = [
        remote(XTo.at[:, shared], XTa.at[rows_of(f), shared], fs.at[0], fr.at[0], core_id),
        remote(XTo.at[:, chunk_of(f ^ 1)], XTa.at[rows_of(f), tail], fs.at[1], fr.at[1], core_id),
        remote(XTo.at[:, shared], XTa.at[rows_of(f), shared], fs.at[2], fr.at[2], x_id),
        remote(XTo.at[:, chunk_of(f ^ 2)], XTa.at[rows_of(f), tail], fs.at[3], fr.at[3], x_id),
        remote(XTo.at[:, chunk_of(f ^ 3)], tmpq, fs.at[4], fr.at[4], x_id),
        remote(XTa.at[rows_of(f ^ 2), shared], XTa.at[rows_of(f ^ 2), shared], fs.at[5], fr.at[5], core_id),
        remote(tmpq, XTa.at[rows_of(f ^ 2), tail], fs.at[6], fr.at[6], core_id),
    ]
    for copy in feats[:5]:
        copy.start()
    XTa[rows_of(f), shared] = XTo[:, shared]
    XTa[rows_of(f), tail] = XTo[:, chunk_of(f)]

    for k in range(2 * S):
        su_ref[k] = 0
    for k in range(7 * S):
        kind_ref[k] = 0

    @pl.loop(0, U)
    def _(u):
        owner = own_ref[u]
        rank = lax.fori_loop(0, u, lambda j, total: total + jnp.where(own_ref[j] == owner, 1, 0), 0)
        distance = owner ^ r
        place = 0
        for bit in range(n):
            place = place + (((distance >> bit) & 1) << (n - 1 - bit))
        pos[u] = place * S + jnp.minimum(rank, S - 1)
        for k in range(2 * S):
            hit = jnp.where(owner == r ^ (k // S), 1, 0) * jnp.where(rank == k % S, 1, 0)
            su_ref[k] = su_ref[k] + hit * u
            here = hit * jnp.where((u % R) // (R // 2) == r % 2, 1, 0)
            late = here * jnp.where(u < R, 1, 0)
            if k < S:
                kind_ref[k] = kind_ref[k] + hit
            kind_ref[S + k] = kind_ref[S + k] + here
            kind_ref[3 * S + k] = kind_ref[3 * S + k] + here - late
            kind_ref[5 * S + k] = kind_ref[5 * S + k] + late

    hyper_arrive(0, 0)
    feats[2].wait_recv()
    feats[4].wait_recv()
    feats[5].start()
    feats[6].start()
    for j in range(1, n - 1):
        hyper_arrive(0, j)
        x_arrive(0, j - 1)
    send_own(1)
    for k in (0, 1, 3, 5, 6):
        feats[k].wait_recv()

    shift0 = small_ref[0:1]
    gain = small_ref[1:2]
    shift = small_ref[2:3]

    def norm(cols):
        h = dot(XTa[:, cols], XTa[:, pl.ds(2 * HALF, D)], TN) + shift0
        mean = jnp.mean(h, axis=-1, keepdims=True)
        cen = h - mean
        rstd = lax.rsqrt(jnp.mean(cen * cen, axis=-1, keepdims=True) + LN_EPS)
        nrm = cen * rstd
        return h, nrm, rstd, (nrm * gain + shift).astype(bf16)

    @pl.loop(0, 8)
    def _(i):
        rows = pl.ds(pl.multiple_of(i * QUART, QUART), QUART)
        h, nrm, rstd, act = norm(rows)
        n1s_ref[rows] = nrm.astype(bf16)
        a1s_ref[rows] = act
        rs_ref[rows] = jnp.broadcast_to(rstd, (QUART, 128))

        @pl.when(i % 4 == f)
        def _():
            h0_ref[pl.ds(pl.multiple_of((i // 4) * 512, 512), QUART)] = h

    hyper_arrive(0, n - 1)
    if n > 1:
        x_arrive(0, n - 2)

    @pl.loop(0, 2)
    def _(t):
        rows = pl.ds(pl.multiple_of(t * QUART, QUART), QUART)
        h, nrm, rstd, act = norm(pl.ds(pl.multiple_of(wide + t * QUART, QUART), QUART))
        n1q_ref[rows] = nrm.astype(bf16)
        a1q_ref[rows] = act
        rq_ref[rows] = jnp.broadcast_to(rstd, (QUART, 128))
        h0_ref[pl.ds(pl.multiple_of(t * 512 + QUART, QUART), QUART)] = h

    XT_ref[...] = XTa[...]
    hyper_arrive(1, 0)
    x_arrive(0, n - 1)
    scale = (HEAD_DIM**-0.5) * LOG2E

    def assemble(p):
        for u in range(U):
            place, rank = pos[u] // S, pos[u] % S
            for k in range(2):
                W[pl.ds(u * BR, BR), pl.ds(p * 256 + k * 128, 128)] = Gs[p][k, place, rank]

    def project(p):
        cols = pl.ds(p * 256, 256)
        for t in range(2):
            sup = pl.multiple_of(t * HALF + f * QUART, QUART)
            wq = W[pl.ds(0, D), cols]
            q_s[pl.ds(t * 512, QUART), cols] = (dot(a1s_ref[pl.ds(sup, QUART)], wq) * scale).astype(bf16)
            q_s[pl.ds(t * 512 + QUART, QUART), cols] = (dot(a1q_ref[pl.ds(t * QUART, QUART)], wq) * scale).astype(bf16)

        @pl.loop(0, 4)
        def _(i):
            rows = pl.ds(pl.multiple_of(i * 512, 512), 512)
            a = a1s_ref[rows]
            k = dot(a, W[pl.ds(D, D), cols]).astype(bf16)
            k_s[rows, cols] = k
            kT_s[cols, rows] = k.T
            v = dot(a, W[pl.ds(2 * D, D), cols]).astype(bf16)
            v_s[rows, cols] = v
            vT_s[cols, rows] = v.T

    def ecopy(i):
        return pltpu.make_async_copy(ET_s.at[i], ET.at[i], esem.at[i])

    def head(h):
        hs = pl.ds(h * HEAD_DIM, HEAD_DIM)

        @pl.loop(0, 2)
        def _(t):
            i = t * HEADS + h
            ks = pl.ds(pl.multiple_of(t * HALF, HALF), HALF)
            qs = pl.ds(pl.multiple_of(t * 512, 512), 512)
            st = dot(k_s[ks, hs], q_s[qs, hs], NT)
            top = jnp.max(st, axis=0, keepdims=True)
            e = jnp.exp2(st - top)
            inv = 1.0 / jnp.sum(e, axis=0, keepdims=True)
            eb = e.astype(bf16)
            ET_s[i] = eb
            ecopy(i).start()
            linv[pl.ds(i, 1)] = inv
            ot = (dot(vT_s[hs, ks], eb) * inv).astype(bf16)
            OT_s[hs, qs] = ot
            O_s[qs, hs] = ot.T

    outs = []

    def ship(src, dst):
        copy = pltpu.make_async_copy(src, dst, osem.at[len(outs)])
        copy.start()
        outs.append(copy)

    all_here(0)
    assemble(0)
    for j in range(1, n - 1):
        hyper_arrive(1, j)
        x_arrive(1, j - 1)
    project(0)
    hyper_arrive(1, n - 1)
    if n > 1:
        x_arrive(1, n - 2)
    head(0)
    x_arrive(1, n - 1)
    head(1)
    all_here(1)
    assemble(1)
    ship(W, Wo)
    project(1)
    ship(q_s, qo)
    ship(kT_s, kTo)
    ship(v_s, vo)
    head(2)
    head(3)
    ship(O_s, Oo)
    ship(OT_s, OT)
    for copy in feats:
        copy.wait_send()
    all_sent(0)
    all_sent(1)
    for i in range(8):
        ecopy(i).wait()
    for copy in outs:
        copy.wait()


def gather_call(R, slots, features, masks, tmap, owners, emb, small):
    S, BR, W = slots.shape
    n = R.bit_length() - 1
    M = n * (n + 1) // 2
    dma = pltpu.SemaphoreType.DMA
    sem = dma((2, len(GROUPS), M))
    sd = jax.ShapeDtypeStruct
    V = pltpu.VMEM
    cols = 2 * HALF + D + 512
    half = V((2, R, S, BR, 128), bf16)
    return pl.pallas_call(
        functools.partial(gather_kernel, R),
        out_shape=(
            sd((2 * S,), jnp.int32), sd((7 * S,), jnp.int32), sd((4 * PADF, cols), bf16), sd((1024, D), f32),
            sd((2048, D), bf16), sd((512, D), bf16), sd((2048, D), bf16), sd((512, D), bf16),
            sd((2048, 128), f32), sd((512, 128), f32), sd((8, 512), f32),
            sd((12 * D, D), bf16), sd((1024, D), bf16), sd((D, 2048), bf16), sd((2048, D), bf16),
            sd((8, HALF, 512), bf16), sd((D, 1024), bf16), sd((1024, D), bf16),
        ),
        in_specs=[vmem(), vmem(), vmem(), smem(), smem(), vmem(), vmem()],
        out_specs=(smem(), smem()) + (vmem(),) * 9 + (anyspace(),) * 7,
        scratch_shapes=[
            pltpu.SMEM(owners.shape, jnp.int32), half, half, V((2, 2, S, BR, 128), bf16),
            V((PADF, 2 * HALF + D + 2048), bf16), V((4 * PADF, cols), bf16), V((PADF, 512), bf16),
            V((12 * D, D), bf16), V((1024, D), bf16), V((2048, D), bf16), V((D, 2048), bf16), V((2048, D), bf16),
            V((D, 2048), bf16), V((8, HALF, 512), bf16), V((D, 1024), bf16), V((1024, D), bf16),
            dma((2,)), dma((6,)), dma((8,)), dma((7,)), dma((7,)),
        ] + [sem] * 8,
        compiler_params=pltpu.CompilerParams(collective_id=0, has_side_effects=True, vmem_limit_bytes=VMEM_BYTES),
        name="gather",
    )(slots, features, masks, tmap, owners, emb, small)


def gelu_pair(u):
    den = 1.0 + (0.3275911 * math.sqrt(0.5)) * jnp.abs(u)
    t = pl.reciprocal(den, approx=True)
    t = t * (2.0 - den * t)
    ex = jnp.exp2((-0.5 * LOG2E) * (u * u))
    poly = t * (0.127414796 + t * (-0.142248368 + t * (0.7107068705 + t * (-0.7265760135 + t * 0.5307027145))))
    e = poly * ex
    phi = jnp.where(u >= 0, 1.0 - e, e)
    return u * phi, phi + u * ex * (1.0 / math.sqrt(2 * math.pi))


AFTER = {
    "fb0": (2, 3), "up": (2,), "mix": (3, 0, 1), "h01": (2,), "h10": (3,), "w0": (2, 0, 3), "h20": (4,),
    "h30": (1, 2, 0, 3), "b0": (4, 2, 1, 0), "b1": (5,), "b2": (3,), "b3": (2,), "b5": (4, 1), "b7": (0, 3), "b9": (4, 5, 1, 0),
}


def main_kernel(
    R, su, occ, linv, small, Wh, Oh, h0h, dYh, ETh, OTh, qh, kTh, vh, a1sh, a1qh, n1sh, n1qh, rsh, rqh, XTh,
    out, FIN, SM, EM, GI,
    W, O_s, y_s, dY, ETb, OT, qs, kT, a1q, n1s, n1q, rs, rq, XT,
    a2_s, G_s, dU_s, Dp, sg, eg, GT, S, RC, RX, RH, AG0, AG1, AGL, SY, RY, SEL, PK, RK, GC, XS, XR,
    lsem, esem, osem, ss, sr, ys, yr, fs, fr, ps, pr, gs, gr,
):
    f = lax.axis_index("feat")
    r = lax.axis_index("rows")
    x = f // 2
    c = f % 2
    n = R.bit_length() - 1
    BH = S.shape[4]
    per = D // (2 * BH)
    core_id = (f ^ 1, r)
    x_id = (f ^ 2, r)
    row_id = [(f, r ^ (1 << j)) for j in range(n)]
    peers = [core_id, x_id] + row_id
    bar = greet(peers)

    loads = {}

    def load(name, src, dst):
        loads[name] = pltpu.make_async_copy(src, dst, lsem.at[len(loads)])
        loads[name].start()

    def rows_w(i):
        return pl.ds(i * D, D)

    load("O", Oh, O_s)
    load("h0", h0h, y_s)
    for i in (3, 4, 8, 5, 9, 6, 10, 7, 11):
        load(i, Wh.at[rows_w(i)], W.at[rows_w(i)])
    load("dY", dYh, dY)
    load("OT", OTh, OT)
    load("q", qh, qs)
    load("kT", kTh, kT)

    def ecopy(h, t):
        k = (h % 2) * 2 + t
        return pltpu.make_async_copy(ETh.at[t * HEADS + h], ETb.at[k], esem.at[k])

    for h in range(2):
        for t in range(2):
            ecopy(h, t).start()
    load("a1q", a1qh, a1q)
    load("n1s", n1sh, n1s)
    load("n1q", n1qh, n1q)
    load("rs", rsh, rs)
    load("rq", rqh, rq)
    load("XT", XTh, XT)
    for i in range(3):
        load(i, Wh.at[rows_w(i)], W.at[rows_w(i)])
    pl.semaphore_wait(bar, len(peers))

    bits = [(r >> j) & 1 for j in range(n)]
    base = [0]
    for j in range(n):
        base.append(base[j] + bits[j] * (R >> (j + 1)))

    def core_copy(g):
        return remote(S.at[1 - c, :, g], RC.at[:, g], ss.at[g, 0], sr.at[g, 0], core_id)

    def x_copy(g):
        return remote(S.at[c, 1 - x, g], RX.at[g], ss.at[g, 1], sr.at[g, 1], x_id)

    def rs_copy(g, j):
        half = R >> (j + 1)
        away = base[j] + (1 - bits[j]) * half
        off = R - (R >> j)
        return remote(
            S.at[c, x, g, pl.ds(away, half)], RH.at[g, pl.ds(off, half)],
            ss.at[g, 2 + j], sr.at[g, 2 + j], row_id[j],
        )

    def swap_copy(g):
        span = pl.ds(base[n - 1], 2)
        return remote(S.at[c, x, g, span], RH.at[g, pl.ds(R - 2, 2)], ss.at[g, 1 + n], sr.at[g, 1 + n], row_id[n - 1])

    def total_of(g):
        return AGL if g == 5 else AG1.at[g // 2] if g % 2 else AG0.at[(g // 2 + 1) % 3]

    def ag_copy(g, j):
        ref = total_of(g).at[pl.ds(base[j + 1] - base[1], R >> (j + 1))]
        return remote(ref, ref, ss.at[g, 2 + n + j], sr.at[g, 2 + n + j], row_id[j])

    def add(a, b):
        return (a.astype(f32) + b.astype(f32)).astype(bf16)

    def step(g, stage):
        if stage == 0:
            core_copy(g).wait_recv()
            S[c, 1 - x, g] = add(S[c, 1 - x, g], RC[1 - x, g])
            x_copy(g).start()
            S[c, x, g] = add(S[c, x, g], RC[x, g])
        elif stage == 1:
            x_copy(g).wait_recv()
            S[c, x, g] = add(S[c, x, g], RX[g])
            rs_copy(g, 0).start()
        elif stage < 1 + n:
            j = stage - 2
            half = R >> (j + 1)
            off = R - (R >> j)
            rs_copy(g, j).wait_recv()
            keep = pl.ds(base[j + 1], half)
            S[c, x, g, keep] = add(S[c, x, g, keep], RH[g, pl.ds(off, half)])
            if j < n - 2:
                rs_copy(g, j + 1).start()
            else:
                swap_copy(g).start()
        elif stage == 1 + n:
            swap_copy(g).wait_recv()
            total_of(g)[pl.ds(base[n - 1] - base[1], 2)] = add(S[c, x, g, pl.ds(base[n - 1], 2)], RH[g, pl.ds(R - 2, 2)])
            if n > 2:
                ag_copy(g, n - 2).start()
        else:
            j = 2 * n - stage
            ag_copy(g, j).wait_recv()
            if j > 1:
                ag_copy(g, j - 1).start()

    def select(m, who):
        picked = []
        for s in range(4):
            u = su[who * 4 + s]
            p = lax.rem(u, R // 2)
            q = lax.div(u, R)
            k = who * 4 + s
            if m == 0:
                picked.append(AG0[q, p].astype(f32) * occ[4 + k].astype(f32))
            else:
                picked.append(AG1[lax.max(q - 1, 0), p].astype(f32) * occ[12 + k].astype(f32) + AGL[p].astype(f32) * occ[20 + k].astype(f32))
        return picked

    def y_copy(m):
        return remote(SY.at[m], RY.at[m], ys.at[m], yr.at[m], row_id[0])

    def fin(m, k):
        if k == 3:
            return pltpu.make_async_copy(SEL.at[m], FIN.at[m, f], osem.at[1 + m])
        src, at = (FIN.at[m, f ^ 2], f ^ 2) if k == 2 else (SEL.at[m], f)
        return remote(src, FIN.at[m, at], fs.at[m, k], fr.at[m, k], x_id if k == 1 else core_id)

    def fin_step(m, stage):
        if stage == 0:
            for s, value in enumerate(select(m, 1)):
                SY[m, s] = value.astype(bf16)
            y_copy(m).start()
            for s, value in enumerate(select(m, 0)):
                SEL[m, s] = value.astype(bf16)
        elif stage == 1:
            y_copy(m).wait_recv()
            SEL[m] = add(SEL[m], RY[m])
            for k in (1, 0, 3):
                fin(m, k).start()
        else:
            fin(m, 1).wait_recv()
            fin(m, 2).start()

    last = 2 * n
    done = [0] * 6
    ended = [0, 0]

    def tick(g):
        if done[g] < last:
            step(g, done[g])
            done[g] += 1

    def finish(m):
        if ended[m] < 3 and all(done[g] == last for g in (m, 2 + m, 4 + m)):
            fin_step(m, ended[m])
            ended[m] += 1

    def after(piece):
        for g in AFTER.get(piece, ()):
            tick(g)

    def put(g0, i, val):
        for k in range(val.shape[1] // 128):
            piece = val[:, k * 128:(k + 1) * 128].reshape(per, 2, BH, 128)
            for h in range(2):
                S[k % 2, h, g0 + k // 2, pl.ds(i * per, per)] = piece[:, h]

    gain2 = small[3:4]
    shift2 = small[4:5]
    RB = 256

    def norm2(y1):
        cen = y1 - jnp.mean(y1, axis=-1, keepdims=True)
        rstd = lax.rsqrt(jnp.mean(cen * cen, axis=-1, keepdims=True) + LN_EPS)
        return cen * rstd, rstd

    loads["O"].wait()
    loads["h0"].wait()
    loads[3].wait()

    @pl.loop(0, 1024 // RB)
    def _(i):
        rows = pl.ds(pl.multiple_of(i * RB, RB), RB)
        y1 = y_s[rows] + dot(O_s[rows], W[rows_w(3)])
        y_s[rows] = y1
        n2, _ = norm2(y1)
        a2 = (n2 * gain2 + shift2).astype(bf16)
        a2_s[rows] = a2
        acc = y1 + small[5:6]
        for j in range(4):
            @pl.when(i == 0)
            def _():
                loads[4 + j].wait()
                loads[8 + j].wait()
            gl, gp = gelu_pair(dot(a2, W[rows_w(4 + j)]) + small[6 + j:7 + j])
            gb = gl.astype(bf16)
            G_s[j, rows] = gb
            dU_s[j, rows] = gp.astype(bf16)
            acc = acc + dot(gb, W[rows_w(8 + j)])
        O_s[rows] = acc.astype(bf16)

    ship_out = pltpu.make_async_copy(O_s, out, osem.at[0])
    ship_out.start()
    loads["dY"].wait()

    @pl.loop(0, 4)
    def _(j):
        put(2, j, dot(G_s[j], dY[...], TN).astype(bf16))

    core_copy(2).start()
    core_copy(3).start()

    sg[...] = jnp.zeros_like(sg)

    def backward_rows(i):
        rows = pl.ds(i * RB, RB)
        dy = dY[rows]
        da2 = jnp.zeros((RB, D), f32)
        for j in range(4):
            du = (dot(dy, W[rows_w(8 + j)], NT) * dU_s[j, rows].astype(f32)).astype(bf16)
            dU_s[j, rows] = du
            sg[6 + j:7 + j] += jnp.sum(du.astype(f32), axis=0, keepdims=True)
            da2 = da2 + dot(du, W[rows_w(4 + j)], NT)
        n2, rstd = norm2(y_s[rows])
        dyf = dy.astype(f32)
        sg[3:4] += jnp.sum(da2 * n2, axis=0, keepdims=True)
        sg[4:5] += jnp.sum(da2, axis=0, keepdims=True)
        sg[5:6] += jnp.sum(dyf, axis=0, keepdims=True)
        cc = da2 * gain2
        m1 = jnp.mean(cc, axis=-1, keepdims=True)
        m2 = jnp.mean(cc * n2, axis=-1, keepdims=True)
        y_s[rows] = dyf + rstd * (cc - m1 - n2 * m2)

    for i in range(1024 // RB):
        backward_rows(i)
        after("fb%d" % i)
    vs = W.at[pl.ds(4 * D, 4 * D)]
    a1s = W.at[pl.ds(8 * D, 4 * D)]
    load("v", vh, vs)
    load("a1s", a1sh, a1s)

    @pl.loop(0, 4)
    def _(j):
        put(0, j, dot(a2_s[...], dU_s[j], TN).astype(bf16))

    core_copy(0).start()
    core_copy(1).start()
    after("up")

    scale = HEAD_DIM**-0.5
    for i in range(2):
        dU_s[1, pl.ds(i * 512, 512)] = y_s[pl.ds(i * 512, 512)].astype(bf16)
    for name in ("OT", "v", "q", "kT", "a1s", "a1q"):
        loads[name].wait()
    put(4, 3, dot(OT[...], dU_s[1]).astype(bf16))

    @pl.loop(0, 2)
    def _(t):
        cols = pl.ds(pl.multiple_of(t * 512, 512), 512)
        whole = dot(W[rows_w(3)], dU_s[1, cols], NT)
        for h in range(HEADS):
            rows = pl.ds(h * HEAD_DIM, HEAD_DIM)
            d = whole[h * HEAD_DIM:(h + 1) * HEAD_DIM] * linv[pl.ds(t * HEADS + h, 1)]
            Dp[pl.ds(t * HEADS + h, 1)] = jnp.sum(d * OT[rows, cols].astype(f32), axis=0, keepdims=True)
            dU_s[2, pl.ds(pl.multiple_of(t * 512 + h * HEAD_DIM, HEAD_DIM), HEAD_DIM)] = d.astype(bf16)

    after("mix")

    def heads(h):
        hs = pl.ds(h * HEAD_DIM, HEAD_DIM)
        for t in range(2):
            ecopy(h, t).wait()

        @pl.loop(0, 2)
        def _(t):
            i = t * HEADS + h
            ksl = pl.ds(pl.multiple_of(t * HALF, HALF), HALF)
            qsl = pl.ds(pl.multiple_of(t * 512, 512), 512)
            do = dU_s[2, pl.ds(pl.multiple_of(t * 512 + h * HEAD_DIM, HEAD_DIM), HEAD_DIM)]
            dp = dot(vs[ksl, hs], do)
            e = ETb[(h % 2) * 2 + t]
            ds = (e.astype(f32) * (dp - Dp[pl.ds(i, 1)])).astype(bf16)
            G_s[2 + t, :, hs] = dot(e, do, NT).astype(bf16)
            G_s[t, :, hs] = (dot(ds, qs[qsl, hs]) * (1.0 / LOG2E)).astype(bf16)
            dqT = (dot(kT[hs, ksl], ds) * scale).astype(bf16)
            dU_s[0, qsl, hs] = dqT.T

        for t in range(2):
            if h + 2 < HEADS:
                ecopy(h + 2, t).start()
            after("h%d%d" % (h, t))

    def weight_grads(m):
        cols = pl.ds(m * 256, 256)
        acc = jnp.zeros((D, 256), f32)
        for t in range(2):
            sup = pl.multiple_of(t * HALF + f * QUART, QUART)
            acc += dot(a1s[pl.ds(sup, QUART)], dU_s[0, pl.ds(t * 512, QUART), cols], TN)
            acc += dot(a1q[pl.ds(t * QUART, QUART)], dU_s[0, pl.ds(t * 512 + QUART, QUART), cols], TN)
        put(4 + m, 0, acc.astype(bf16))
        for k in range(2):
            total = dot(a1s[pl.ds(0, HALF)], G_s[2 * k, :, cols], TN) + dot(a1s[pl.ds(HALF, HALF)], G_s[2 * k + 1, :, cols], TN)
            put(4 + m, 1 + k, total.astype(bf16))

    for m in range(2):
        heads(2 * m)
        heads(2 * m + 1)
        weight_grads(m)
        core_copy(4 + m).start()
        after("w%d" % m)

    eg[...] = jnp.zeros_like(eg)
    gain1 = small[1:2]
    emb_cols = pl.ds(2 * HALF, D)
    for name in ("n1s", "n1q", "rs", "rq", "XT", 0, 1, 2):
        loads[name].wait()

    def back(da, nrm, rstd, extra, cols, out_cols):
        sg[1:2] += jnp.sum(da * nrm, axis=0, keepdims=True)
        sg[2:3] += jnp.sum(da, axis=0, keepdims=True)
        cc = da * gain1
        m1 = jnp.mean(cc, axis=-1, keepdims=True)
        m2 = jnp.mean(cc * nrm, axis=-1, keepdims=True)
        wide = jnp.concatenate([rstd] * 4, axis=1)
        dh = wide * (cc - m1 - nrm * m2)
        if extra is not None:
            dh = dh + extra
        sg[0:1] += jnp.sum(dh, axis=0, keepdims=True)
        de = dh.astype(bf16)
        part = dot(XT[:, cols], de)
        back_in = dot(XT[:, emb_cols], de, NT).astype(bf16)
        for k in range(4):
            eg[k] += part[k * PADF:(k + 1) * PADF]
            GT[k % 2, k // 2, :, out_cols] = back_in[k * PADF:(k + 1) * PADF]

    def below(t):
        q0 = t * 512
        wq, wk, wv = W[rows_w(0)], W[rows_w(1)], W[rows_w(2)]
        da = dot(dU_s[0, pl.ds(q0 + QUART, QUART)], wq, NT)
        p0 = pl.ds(t * QUART, QUART)
        back(
            da, n1q[p0].astype(f32), rq[p0], y_s[pl.ds(q0 + QUART, QUART)],
            pl.ds(2 * HALF + D + t * QUART, QUART), pl.ds(2 * HALF + t * QUART, QUART),
        )
        after("b%d" % (5 * t))
        for b in range(4):
            at = pl.ds(pl.multiple_of(((f + b) % 4) * QUART, QUART), QUART)
            rows = pl.ds(pl.multiple_of(t * HALF + ((f + b) % 4) * QUART, QUART), QUART)
            da = dot(G_s[t, at], wk, NT) + dot(G_s[2 + t, at], wv, NT)
            extra = None
            if b == 0:
                da = da + dot(dU_s[0, pl.ds(q0, QUART)], wq, NT)
                extra = y_s[pl.ds(q0, QUART)]
            back(da, n1s[rows].astype(f32), rs[rows], extra, rows, rows)
            if 5 * t + b < 8:
                after("b%d" % (5 * t + b + 1))

    below(0)
    below(1)

    small_rows = pl.ds(0, 16)
    PK[0, small_rows] = sg[...]
    for k in range(2):
        PK[0, pl.ds(16 + k * PADF, PADF)] = eg[2 * k + 1 - c]

    def pk_copy(i):
        rows = pl.ds(0, 80 if i == 0 else 48)
        dev = core_id if i == 0 else x_id if i == 1 else row_id[i - 2]
        return remote(PK.at[i, rows], RK.at[i, rows], ps.at[i], pr.at[i], dev)

    def pk_step(i):
        pk_copy(i).wait_recv()
        if i == 0:
            PK[1, small_rows] = PK[0, small_rows] + RK[0, small_rows]
            own = [eg[2 * k + c] + RK[0, pl.ds(16 + k * PADF, PADF)] for k in range(2)]
            PK[1, pl.ds(16, PADF)] = jnp.where(x == 0, own[1], own[0])
            PK[1, pl.ds(48, PADF)] = jnp.where(x == 0, own[0], own[1])
            pk_copy(1).start()
        else:
            old = PK[1, pl.ds(48, PADF)] if i == 1 else PK[i, pl.ds(16, PADF)]
            a = PK[i, small_rows] + RK[i, small_rows]
            b = old + RK[i, pl.ds(16, PADF)]
            if i < n + 1:
                PK[i + 1, small_rows] = a
                PK[i + 1, pl.ds(16, PADF)] = b
                pk_copy(i + 1).start()
            else:
                SM[...] = a
                EM[...] = b

    pk_copy(0).start()
    gt1 = remote(GT.at[1 - c], GC, gs.at[0], gr.at[0], core_id)
    gt1.start()
    sup = pl.ds(0, 2 * HALF)
    que = pl.ds(2 * HALF, 512)

    def que_of(k):
        return pl.ds(pl.multiple_of(2 * HALF + k * 512, 512), 512)

    gt2 = remote(XS, XR, gs.at[1], gr.at[1], x_id)
    after("b9")
    pk_step(0)
    gt1.wait_recv()
    XS[:, sup] = add(GT[c, 1 - x, :, sup], GC[1 - x, :, sup])
    XS[:, que_of(c)] = GT[c, 1 - x, :, que]
    XS[:, que_of(1 - c)] = GC[1 - x, :, que]
    gt2.start()
    next_pk = 1
    while min(done) < last:
        for g in (4, 5, 2, 3, 1, 0):
            tick(g)
        finish(0)
        if next_pk < n + 2:
            pk_step(next_pk)
            next_pk += 1
    finish(1)
    finish(0)
    for i in range(next_pk, n + 2):
        pk_step(i)
    gt2.wait_recv()
    GI[:, sup] = (
        GT[c, x, :, sup].astype(f32) + GC[x, :, sup].astype(f32) + XR[:, sup].astype(f32)
    ).astype(bf16)
    GI[:, que_of(f)] = GT[c, x, :, que]
    GI[:, que_of(f ^ 1)] = GC[x, :, que]
    for k in range(2):
        GI[:, que_of(2 * (1 - x) + k)] = XR[:, pl.ds(2 * HALF + k * 512, 512)]
    while min(ended) < 3:
        finish(0)
        finish(1)
    for m in range(2):
        y_copy(m).wait_send()
        fin(m, 0).wait()
        fin(m, 1).wait_send()
        fin(m, 2).wait()
        fin(m, 3).wait()
    for g in range(6):
        core_copy(g).wait_send()
        x_copy(g).wait_send()
        swap_copy(g).wait_send()
        for j in range(n - 1):
            rs_copy(g, j).wait_send()
        for j in range(1, n - 1):
            ag_copy(g, j).wait_send()
    for i in range(n + 2):
        pk_copy(i).wait_send()
    gt1.wait_send()
    gt2.wait_send()
    ship_out.wait()


def main_call(R, su, occ, linv, small, W, O, h0, dY, ET, OT, q, kT, v, a1s, a1q, n1s, n1q, rs, rq, XT):
    BH = 12 * D // (3 * R) // 2
    n = R.bit_length() - 1
    sd = jax.ShapeDtypeStruct
    V = pltpu.VMEM
    dma = pltpu.SemaphoreType.DMA
    blk = (R, BH, 128)
    like = lambda a: V(a.shape, a.dtype)
    return pl.pallas_call(
        functools.partial(main_kernel, R),
        out_shape=(sd((1024, D), bf16), sd((2, 4, 4, BH, 128), bf16), sd((16, D), f32), sd((PADF, D), f32), sd((PADF, 4096), bf16)),
        in_specs=[smem(), smem(), vmem(), vmem()] + [anyspace()] * 16,
        out_specs=(anyspace(), anyspace(), vmem(), vmem(), vmem()),
        scratch_shapes=[
            like(W), like(O), like(h0), like(dY), V((4, HALF, 512), bf16), like(OT), like(q), like(kT),
            like(a1q), like(n1s), like(n1q), like(rs), like(rq), like(XT),
            V((1024, D), bf16), V((4, 1024, 512), bf16), V((4, 1024, 512), bf16), V((8, 512), f32), V((16, D), f32),
            V((4, PADF, D), f32), V((2, 2, PADF, 2560), bf16),
            V((2, 2, 6) + blk, bf16), V((2, 6) + blk, bf16), V((6,) + blk, bf16), V((6,) + blk, bf16), V((3, R // 2, BH, 128), bf16), V((2, R // 2, BH, 128), bf16), V((R // 2, BH, 128), bf16),
            V((2, 4, BH, 128), bf16), V((2, 4, BH, 128), bf16), V((2, 4, BH, 128), bf16), V((n + 2, 80, D), f32), V((n + 2, 80, D), f32),
            V((2, PADF, 2560), bf16), V((PADF, 3072), bf16), V((PADF, 3072), bf16),
            dma((26,)), dma((4,)), dma((3,)), dma((6, 2 + 2 * n)), dma((6, 2 + 2 * n)), dma((2,)), dma((2,)), dma((2, 3)), dma((2, 3)),
            dma((n + 2,)), dma((n + 2,)), dma((2,)), dma((2,)),
        ],
        compiler_params=pltpu.CompilerParams(collective_id=1, has_side_effects=True, vmem_limit_bytes=VMEM_BYTES),
        name="main",
    )(su, occ, linv, small, W, O, h0, dY, ET, OT, q, kT, v, a1s, a1q, n1s, n1q, rs, rq, XT)


def adamw(weight, grad, first, second, rate):
    first_new = BETA_FIRST * first + (1.0 - BETA_FIRST) * grad
    second_new = BETA_SECOND * second + (1.0 - BETA_SECOND) * grad * grad
    first_hat = first_new / (1.0 - BETA_FIRST**STEP)
    second_hat = second_new / (1.0 - BETA_SECOND**STEP)
    weight_new = weight - rate * (first_hat / (jnp.sqrt(second_hat) + ADAM_EPS) + DECAY * weight)
    return (first_new, second_new, weight_new)


def update_kernel(
    occ, tmap, FIN, w, m, v, SM, sw, sm, sv, EM, ew, em, ev, GI, masks, lo,
    g_o, m_o, v_o, w_o, wc_o, eg_o, em_o, ev_o, ew_o, ec_o, sg_o, sm_o, sv_o, sw_o, gi_o, lo_o,
):
    s = pl.program_id(0)
    keep = occ[s].astype(f32)
    BH = FIN.shape[3]
    for f in range(4):
        rows = pl.ds((f // 2) * BH, BH)
        for k in range(2):
            cols = pl.ds(k * 256 + (f % 2) * 128, 128)
            g = FIN[k, f, 0].astype(f32)
            a, b, d = adamw(w[0, rows, cols], g, m[0, rows, cols], v[0, rows, cols], RATE_MATRIX)
            g_o[0, rows, cols] = g * keep
            m_o[0, rows, cols] = a * keep
            v_o[0, rows, cols] = b * keep
            d = d * keep
            w_o[0, rows, cols] = d
            wc_o[0, rows, cols] = d.astype(bf16)

    @pl.when(s == 0)
    def _():
        g = SM[0:10]
        a, b, d = adamw(sw[...], g, sm[...], sv[...], RATE_SMALL)
        sg_o[...] = g
        sm_o[...] = a
        sv_o[...] = b
        sw_o[...] = d
        nf = ew.shape[0]
        g = EM[pl.ds(0, nf)]
        a, b, d = adamw(ew[...], g, em[...], ev[...], RATE_EMBED)
        eg_o[...] = g
        em_o[...] = a
        ev_o[...] = b
        ew_o[...] = d
        ec_o[...] = d.astype(bf16)

    nf = gi_o.shape[1]
    t = s // 2
    keep_in = mask_column(masks, tmap[t])

    @pl.when(s % 2 == 0)
    def _():
        cols = pl.ds(pl.multiple_of(t * HALF, HALF), HALF)
        gi_o[t, :, 0, :] = (GI[pl.ds(0, nf), cols].astype(f32) * keep_in).astype(bf16)

    @pl.when(s % 2 == 1)
    def _():
        for k in range(4):
            cols = pl.ds(pl.multiple_of(2 * HALF + k * 512 + t * QUART, QUART), QUART)
            gi_o[t, :, 1, pl.ds(k * QUART, QUART)] = (GI[pl.ds(0, nf), cols].astype(f32) * keep_in).astype(bf16)

    lo_o[...] = lo[...]


def update_call(occ, tmap, FIN, w, m, v, SM, sw, sm, sv, EM, ew, em, ev, GI, masks, lo):
    S, BR, W = w.shape
    nf = ew.shape[0]
    sd = jax.ShapeDtypeStruct
    blk = pl.BlockSpec((1, BR, W), lambda s: (s, 0, 0))
    whole = lambda a: pl.BlockSpec(a.shape, lambda s: (0,) * len(a.shape))
    ins = [smem(), smem(), pl.BlockSpec((2, 4, 1, BR // 2, 128), lambda s: (0, 0, s, 0, 0)), blk, blk, blk]
    ins += [whole(a) for a in (SM, sw, sm, sv, EM, ew, em, ev, GI, masks)] + [pl.BlockSpec((1024 // S, D), lambda s: (s, 0))]
    big = sd((S, BR, W), f32)
    small = sd((10, D), f32)
    e = sd((nf, D), f32)
    outs = [big, big, big, big, sd((S, BR, W), bf16), e, e, e, e, sd((nf, D), bf16), small, small, small, small, sd((2, nf, 2, HALF), bf16), sd(lo.shape, lo.dtype)]
    specs = [blk] * 5 + [whole(a) for a in outs[5:14]] + [whole(outs[14]), pl.BlockSpec((1024 // S, D), lambda s: (s, 0))]
    return pl.pallas_call(
        update_kernel, out_shape=tuple(outs), grid=(S,), in_specs=ins, out_specs=tuple(specs),
        compiler_params=pltpu.CompilerParams(vmem_limit_bytes=VMEM_BYTES), name="update",
    )(occ, tmap, FIN, w, m, v, SM, sw, sm, sv, EM, ew, em, ev, GI, masks, lo)


def body(
    features, feature_masks, table_map, owners, out_grad, weight_slots, moment1_slots, moment2_slots,
    emb_weight, emb_moment1, emb_moment2, small_weight, small_moment1, small_moment2,
):
    width = weight_slots.shape[2]
    R = lax.axis_size("rows")
    slot_unit, kinds, XT, h0o, a1s, a1q, n1s, n1q, rs, rq, linv, W, q, kT, v, ET, OT, O = gather_call(
        R, weight_slots, features.transpose(0, 3, 1, 2), feature_masks, table_map, owners, emb_weight, small_weight
    )
    dY = out_grad.reshape(1024, width)
    out, FIN, SM, EM, GI = main_call(
        R, slot_unit, kinds, linv, small_weight, W, O, h0o, dY, ET, OT, q, kT, v, a1s, a1q, n1s, n1q, rs, rq, XT
    )
    (
        g_slots, m_slots, v_slots, w_slots, w_copy, e_grad, e_m, e_v, e_w, e_copy, s_grad, s_m, s_v, s_w, grad_inputs, out,
    ) = update_call(
        kinds, table_map, FIN, weight_slots, moment1_slots, moment2_slots, SM, small_weight, small_moment1,
        small_moment2, EM, emb_weight, emb_moment1, emb_moment2, GI, feature_masks, out,
    )
    grad_inputs = grad_inputs.transpose(0, 2, 3, 1)
    return (
        out.reshape(out_grad.shape), grad_inputs, g_slots, m_slots, v_slots, w_slots, w_copy,
        e_grad, e_m, e_v, e_w, e_copy, s_grad, s_m, s_v, s_w,
    )


def solution(mesh):
    rows3 = P("rows", None, None)
    feat2 = P("feat", None)
    in_specs = (
        P("rows", None, None, "feat"), P(None, "feat"), P("rows"), P(), P("rows", None, "feat", None),
        rows3, rows3, rows3, feat2, feat2, feat2, P(), P(), P(),
    )
    out_specs = (
        P("rows", None, "feat", None), P("rows", None, None, "feat"), rows3, rows3, rows3, rows3, rows3,
        feat2, feat2, feat2, feat2, feat2, P(), P(), P(), P(),
    )
    return jax.shard_map(body, mesh=mesh, in_specs=in_specs, out_specs=out_specs, check_vma=False)
```

profile of v0, /device:TPU:0, one launch (start us, length us, event | category | flops | bytes accessed | tf_op | source)
XLA Modules:
  0.0 170.1 jit_solution(4125312114597920113)
XLA Ops:
  0.6 65.1 %gather.1 = (s32[8]{0:T(128)}, s32[28]{0:T(128)}, bf16[128,3072]{1,0:T(8,128)(2,1)}, f32[1024,512]{1,0:T(8,128)}, bf16[2048,512]{1,0:T(8,128)(2,1)}, /*index=5*/...) custom-call(f32[4,256,512]{2,1,0:T(8,128)} %w.1, ...), custom_call_target="tpu_custom_call" | custom-call | tf_op jit(solution)/shard_map/gather/pallas_call | solution.py:392
  65.8 94.8 %main.1 = (bf16[1024,512]{1,0:T(8,128)(2,1)}, bf16[2,4,4,128,128]{4,3,2,1,0:T(8,128)(2,1)}, f32[16,512]{1,0:T(8,128)}, f32[32,512]{1,0:T(8,128)}, bf16[32,4096]{1,0:T(8,128)(2,1)}) custom-call(s32[8]{0:T(128)} %get-tuple-element.56.su, s32[28]{0:T(128)} %get-tuple-element.55.occ, f32[8,512]{1,0:T(8,128)} %get-tuple-element.57.linv, f32[10,512]{1,0:T(8,128)} %sw.1, ...), custom_call_target="tpu_custom_call" | custom-call | tf_op jit(solution)/shard_map/main/pallas_call | solution.py:907
  160.6 9.3 %update.1 = (f32[4,256,512]{2,1,0:T(8,128)}, f32[4,256,512]{2,1,0:T(8,128)}, f32[4,256,512]{2,1,0:T(8,128)}, f32[4,256,512]{2,1,0:T(8,128)}, bf16[4,256,512]{2,1...) custom-call(s32[28]{0:T(128)} %get-tuple-element.55.occ, ...), custom_call_target="tpu_custom_call" | custom-call | tf_op jit(solution)/shard_map/update/pallas_call | solution.py:1005
where the time goes:
time: 170 us
  Pallas kernels  169 us (99%)
    pallas_call x1, Pallas kernels, main_call(): pl.pallas_call(functools.partial(main_kernel, R), out_shape=(sd((1024, D)...  94.8 us
    pallas_call x1, Pallas kernels, gather_call(): pl.pallas_call(functools.partial(gather_kernel, R), out_shape=(sd((2 * S,...  65.1 us
    pallas_call x1, Pallas kernels, update_call(): pl.pallas_call(update_kernel, out_shape=tuple(outs), grid=(S,), in_specs=...  9.29 us

commit v1 on v0

--- a/solution.py
+++ b/solution.py
@@ -928,8 +928,8 @@
 def adamw(weight, grad, first, second, rate):
     first_new = BETA_FIRST * first + (1.0 - BETA_FIRST) * grad
     second_new = BETA_SECOND * second + (1.0 - BETA_SECOND) * grad * grad
-    first_hat = first_new / (1.0 - BETA_FIRST**STEP)
-    second_hat = second_new / (1.0 - BETA_SECOND**STEP)
+    first_hat = first_new * (1.0 / (1.0 - BETA_FIRST**STEP))
+    second_hat = second_new * (1.0 / (1.0 - BETA_SECOND**STEP))
     weight_new = weight - rate * (first_hat / (jnp.sqrt(second_hat) + ADAM_EPS) + DECAY * weight)
     return (first_new, second_new, weight_new)
 
@@ -939,20 +939,21 @@
     g_o, m_o, v_o, w_o, wc_o, eg_o, em_o, ev_o, ew_o, ec_o, sg_o, sm_o, sv_o, sw_o, gi_o, lo_o,
 ):
     s = pl.program_id(0)
-    keep = occ[s].astype(f32)
     BH = FIN.shape[3]
-    for f in range(4):
-        rows = pl.ds((f // 2) * BH, BH)
-        for k in range(2):
-            cols = pl.ds(k * 256 + (f % 2) * 128, 128)
-            g = FIN[k, f, 0].astype(f32)
-            a, b, d = adamw(w[0, rows, cols], g, m[0, rows, cols], v[0, rows, cols], RATE_MATRIX)
-            g_o[0, rows, cols] = g * keep
-            m_o[0, rows, cols] = a * keep
-            v_o[0, rows, cols] = b * keep
-            d = d * keep
-            w_o[0, rows, cols] = d
-            wc_o[0, rows, cols] = d.astype(bf16)
+    for slot in range(2):
+        keep = occ[2 * s + slot].astype(f32)
+        for f in range(4):
+            rows = pl.ds((f // 2) * BH, BH)
+            for k in range(2):
+                cols = pl.ds(k * 256 + (f % 2) * 128, 128)
+                g = FIN[k, f, slot].astype(f32)
+                a, b, d = adamw(w[slot, rows, cols], g, m[slot, rows, cols], v[slot, rows, cols], RATE_MATRIX)
+                g_o[slot, rows, cols] = g * keep
+                m_o[slot, rows, cols] = a * keep
+                v_o[slot, rows, cols] = b * keep
+                d = d * keep
+                w_o[slot, rows, cols] = d
+                wc_o[slot, rows, cols] = d.astype(bf16)
 
     @pl.when(s == 0)
     def _():
@@ -972,19 +973,13 @@
         ec_o[...] = d.astype(bf16)
 
     nf = gi_o.shape[1]
-    t = s // 2
+    t = s
     keep_in = mask_column(masks, tmap[t])
-
-    @pl.when(s % 2 == 0)
-    def _():
-        cols = pl.ds(pl.multiple_of(t * HALF, HALF), HALF)
-        gi_o[t, :, 0, :] = (GI[pl.ds(0, nf), cols].astype(f32) * keep_in).astype(bf16)
-
-    @pl.when(s % 2 == 1)
-    def _():
-        for k in range(4):
-            cols = pl.ds(pl.multiple_of(2 * HALF + k * 512 + t * QUART, QUART), QUART)
-            gi_o[t, :, 1, pl.ds(k * QUART, QUART)] = (GI[pl.ds(0, nf), cols].astype(f32) * keep_in).astype(bf16)
+    cols = pl.ds(pl.multiple_of(t * HALF, HALF), HALF)
+    gi_o[t, :, 0, :] = (GI[pl.ds(0, nf), cols].astype(f32) * keep_in).astype(bf16)
+    for k in range(4):
+        cols = pl.ds(pl.multiple_of(2 * HALF + k * 512 + t * QUART, QUART), QUART)
+        gi_o[t, :, 1, pl.ds(k * QUART, QUART)] = (GI[pl.ds(0, nf), cols].astype(f32) * keep_in).astype(bf16)
 
     lo_o[...] = lo[...]
 
@@ -993,17 +988,17 @@
     S, BR, W = w.shape
     nf = ew.shape[0]
     sd = jax.ShapeDtypeStruct
-    blk = pl.BlockSpec((1, BR, W), lambda s: (s, 0, 0))
+    blk = pl.BlockSpec((2, BR, W), lambda s: (s, 0, 0))
     whole = lambda a: pl.BlockSpec(a.shape, lambda s: (0,) * len(a.shape))
-    ins = [smem(), smem(), pl.BlockSpec((2, 4, 1, BR // 2, 128), lambda s: (0, 0, s, 0, 0)), blk, blk, blk]
-    ins += [whole(a) for a in (SM, sw, sm, sv, EM, ew, em, ev, GI, masks)] + [pl.BlockSpec((1024 // S, D), lambda s: (s, 0))]
+    ins = [smem(), smem(), pl.BlockSpec((2, 4, 2, BR // 2, 128), lambda s: (0, 0, s, 0, 0)), blk, blk, blk]
+    ins += [whole(a) for a in (SM, sw, sm, sv, EM, ew, em, ev, GI, masks)] + [pl.BlockSpec((2048 // S, D), lambda s: (s, 0))]
     big = sd((S, BR, W), f32)
     small = sd((10, D), f32)
     e = sd((nf, D), f32)
     outs = [big, big, big, big, sd((S, BR, W), bf16), e, e, e, e, sd((nf, D), bf16), small, small, small, small, sd((2, nf, 2, HALF), bf16), sd(lo.shape, lo.dtype)]
-    specs = [blk] * 5 + [whole(a) for a in outs[5:14]] + [whole(outs[14]), pl.BlockSpec((1024 // S, D), lambda s: (s, 0))]
+    specs = [blk] * 5 + [whole(a) for a in outs[5:14]] + [whole(outs[14]), pl.BlockSpec((2048 // S, D), lambda s: (s, 0))]
     return pl.pallas_call(
-        update_kernel, out_shape=tuple(outs), grid=(S,), in_specs=ins, out_specs=tuple(specs),
+        update_kernel, out_shape=tuple(outs), grid=(S // 2,), in_specs=ins, out_specs=tuple(specs),
         compiler_params=pltpu.CompilerParams(vmem_limit_bytes=VMEM_BYTES), name="update",
     )(occ, tmap, FIN, w, m, v, SM, sw, sm, sv, EM, ew, em, ev, GI, masks, lo)
 

time: 170 us -> 169 us (level)
  no operation moved by 1% of the time
where the time goes in v1:
time: 169 us
  Pallas kernels  168 us (99%)
    pallas_call x1, Pallas kernels, main_call(): pl.pallas_call(functools.partial(main_kernel, R), out_shape=(sd((1024, D)...  94.8 us
    pallas_call x1, Pallas kernels, gather_call(): pl.pallas_call(functools.partial(gather_kernel, R), out_shape=(sd((2 * S,...  65.1 us
    pallas_call x1, Pallas kernels, update_call(): pl.pallas_call(update_kernel, out_shape=tuple(outs), grid=(S // 2,), in_s...  7.94 us

profile of v1, /device:TPU:0, one launch (start us, length us, event | category | flops | bytes accessed | tf_op | source)
XLA Modules:
  0.0 168.7 jit_solution(4084853193307282690)
XLA Ops:
  0.6 65.1 %gather.1 = (s32[8]{0:T(128)}, s32[28]{0:T(128)}, bf16[128,3072]{1,0:T(8,128)(2,1)}, f32[1024,512]{1,0:T(8,128)}, bf16[2048,512]{1,0:T(8,128)(2,1)}, /*index=5*/...) custom-call(f32[4,256,512]{2,1,0:T(8,128)} %w.1, ...), custom_call_target="tpu_custom_call" | custom-call | tf_op jit(solution)/shard_map/gather/pallas_call | solution.py:392
  65.8 94.8 %main.1 = (bf16[1024,512]{1,0:T(8,128)(2,1)}, bf16[2,4,4,128,128]{4,3,2,1,0:T(8,128)(2,1)}, f32[16,512]{1,0:T(8,128)}, f32[32,512]{1,0:T(8,128)}, bf16[32,4096]{1,0:T(8,128)(2,1)}) custom-call(s32[8]{0:T(128)} %get-tuple-element.56.su, s32[28]{0:T(128)} %get-tuple-element.55.occ, f32[8,512]{1,0:T(8,128)} %get-tuple-element.57.linv, f32[10,512]{1,0:T(8,128)} %sw.1, ...), custom_call_target="tpu_custom_call" | custom-call | tf_op jit(solution)/shard_map/main/pallas_call | solution.py:907
  160.6 7.9 %update.1 = (f32[4,256,512]{2,1,0:T(8,128)}, f32[4,256,512]{2,1,0:T(8,128)}, f32[4,256,512]{2,1,0:T(8,128)}, f32[4,256,512]{2,1,0:T(8,128)}, bf16[4,256,512]{2,1...) custom-call(s32[28]{0:T(128)} %get-tuple-element.55.occ, ...), custom_call_target="tpu_custom_call" | custom-call | tf_op jit(solution)/shard_map/update/pallas_call | solution.py:1000

commit v2 on v1

--- a/solution.py
+++ b/solution.py
@@ -245,7 +245,6 @@
     for j in range(1, n - 1):
         hyper_arrive(0, j)
         x_arrive(0, j - 1)
-    send_own(1)
     for k in (0, 1, 3, 5, 6):
         feats[k].wait_recv()
 
@@ -261,8 +260,7 @@
         nrm = cen * rstd
         return h, nrm, rstd, (nrm * gain + shift).astype(bf16)
 
-    @pl.loop(0, 8)
-    def _(i):
+    def support_rows(i):
         rows = pl.ds(pl.multiple_of(i * QUART, QUART), QUART)
         h, nrm, rstd, act = norm(rows)
         n1s_ref[rows] = nrm.astype(bf16)
@@ -273,6 +271,9 @@
         def _():
             h0_ref[pl.ds(pl.multiple_of((i // 4) * 512, 512), QUART)] = h
 
+    pl.loop(0, 4)(support_rows)
+    send_own(1)
+    pl.loop(4, 8)(support_rows)
     hyper_arrive(0, n - 1)
     if n > 1:
         x_arrive(0, n - 2)
@@ -346,11 +347,11 @@
         copy.start()
         outs.append(copy)
 
-    all_here(0)
-    assemble(0)
     for j in range(1, n - 1):
         hyper_arrive(1, j)
         x_arrive(1, j - 1)
+    all_here(0)
+    assemble(0)
     project(0)
     hyper_arrive(1, n - 1)
     if n > 1:

time: 169 us -> 168 us (level)
  Pallas kernels: 168 us -> 166 us
where the time goes in v2:
time: 168 us; the launch traced here: 167 us
  Pallas kernels  166 us (99%)
    pallas_call x1, Pallas kernels, main_call(): pl.pallas_call(functools.partial(main_kernel, R), out_shape=(sd((1024, D)...  93.8 us
    pallas_call x1, Pallas kernels, gather_call(): pl.pallas_call(functools.partial(gather_kernel, R), out_shape=(sd((2 * S,...  64.7 us
    pallas_call x1, Pallas kernels, update_call(): pl.pallas_call(update_kernel, out_shape=tuple(outs), grid=(S // 2,), in_s...  7.94 us

profile of v2, /device:TPU:0, one launch (start us, length us, event | category | flops | bytes accessed | tf_op | source)
XLA Modules:
  0.0 167.3 jit_solution(7403157732802984615)
XLA Ops:
  0.6 64.7 %gather.1 = (s32[8]{0:T(128)}, s32[28]{0:T(128)}, bf16[128,3072]{1,0:T(8,128)(2,1)}, f32[1024,512]{1,0:T(8,128)}, bf16[2048,512]{1,0:T(8,128)(2,1)}, /*index=5*/...) custom-call(f32[4,256,512]{2,1,0:T(8,128)} %w.1, ...), custom_call_target="tpu_custom_call" | custom-call | tf_op jit(solution)/shard_map/gather/pallas_call | solution.py:393
  65.4 93.8 %main.1 = (bf16[1024,512]{1,0:T(8,128)(2,1)}, bf16[2,4,4,128,128]{4,3,2,1,0:T(8,128)(2,1)}, f32[16,512]{1,0:T(8,128)}, f32[32,512]{1,0:T(8,128)}, bf16[32,4096]{1,0:T(8,128)(2,1)}) custom-call(s32[8]{0:T(128)} %get-tuple-element.56.su, s32[28]{0:T(128)} %get-tuple-element.55.occ, f32[8,512]{1,0:T(8,128)} %get-tuple-element.57.linv, f32[10,512]{1,0:T(8,128)} %sw.1, ...), custom_call_target="tpu_custom_call" | custom-call | tf_op jit(solution)/shard_map/main/pallas_call | solution.py:908
  159.2 7.9 %update.1 = (f32[4,256,512]{2,1,0:T(8,128)}, f32[4,256,512]{2,1,0:T(8,128)}, f32[4,256,512]{2,1,0:T(8,128)}, f32[4,256,512]{2,1,0:T(8,128)}, bf16[4,256,512]{2,1...) custom-call(s32[28]{0:T(128)} %get-tuple-element.55.occ, ...), custom_call_target="tpu_custom_call" | custom-call | tf_op jit(solution)/shard_map/update/pallas_call | solution.py:1001
